TPU v7x, 32 devices: a whole 2x2x4 slice. The times are simulated.
32 devices in a mesh: groups: 2 (over y), req: 4 (over x, core), tensor: 4 (over z).
Axes of the slice: x: 2, y: 2, z: 4, core: 2. Of those that a mesh axis runs over, the one named last changes fastest.
Arguments:
- hidden: bfloat16 [384, 24576], P(('groups', 'req'), 'tensor'), parts along dimension 0, may hold values from -6 to 6
- join_weight: bfloat16 [24576, 8192], P('tensor', 'req'), may hold values from -0.0390625 to 0.0390625
- norm_gain: bfloat16 [8192], P(('req', 'tensor')), may hold values from 0.099609375 to 1.8984375
- qkv_weight: bfloat16 [8192, 9216], P(('req', 'tensor')), may hold values from -0.0625 to 0.0625
- owner_draft_cache: bfloat16 [48, 512, 2, 512], P(('groups', 'req'), 'tensor'), parts along dimension 0, may hold values from -250 to 250
- node_count: int32 [48], P('groups'), parts along dimension 0, may hold values from 1 to 8, as said below
- owner: int32 [48], P('groups'), parts along dimension 0, may hold values from 0 to 3, as said below
- cache_len: int32 [48], P('groups'), parts along dimension 0, may hold values from 1 to 512, as said below
Outputs:
- draft_attention: bfloat16 [48, 8, 8192], P(('groups', 'req'), None, 'tensor'), parts along dimension 0
There are 2 independent parts, one for each index of `groups`. A program takes and returns all parts, laid end to end along the dimension named above; an argument that names none is the same for every part. Nothing has to cross between parts.
Inputs may be any that keep to these rules, and one draw needn't show every extreme that they name: Every owner holds exactly 6 requests. `node_count`: some request has all 8 nodes live. `cache_len`: some slot uses all 512 positions.
All inputs are finite; a program needn't handle non-finite values.
Results may differ from a plain program's by a relative error of at most 0.01655.
The roundings to bfloat16 on the way count: a program that leaves them out, or rounds other values in their place, can miss the bound.
Values may be sent and summed in bfloat16 or wider, within the bound.
A program may use at most 256 MiB of HBM per device.

v0:
```python
import jax
import jax.numpy as jnp
from jax import lax
from jax.sharding import PartitionSpec as P

DF = 8192
QUERY_HEADS = 64
KEY_VALUE_HEADS = 4
HEAD_SIZE = 128
TREE_SLOTS = 8
CACHE_BLOCK = 128
norm_eps = 1e-05


def slots(owner, request_per_owner):
    count_all = owner.shape[0]
    same_owner = owner[:, None] == owner[None, :]
    earlier = jnp.arange(count_all)[None, :] < jnp.arange(count_all)[:, None]
    ranking = jnp.sum((same_owner & earlier).astype(jnp.int32), axis=1)
    return owner * request_per_owner + ranking


def body(
    hidden, join_weight, norm_gain, qkv_weight, owner_draft_cache, node_count, owner, cache_len
):
    tensor_count = lax.axis_size("tensor")
    req_here = lax.axis_index("req")
    tensor_here = lax.axis_index("tensor")
    request_per_owner = owner_draft_cache.shape[0]
    count_all = owner.shape[0]
    slot_of = slots(owner, request_per_owner)
    slot_table = slot_of[None, :] == jnp.arange(count_all, dtype=jnp.int32)[:, None]
    rows_all = count_all * TREE_SLOTS
    hidden_all = lax.all_gather(hidden, "req", axis=0, tiled=True)
    partial_sum = jnp.dot(hidden_all, join_weight, preferred_element_type=jnp.float32)
    joined = lax.psum_scatter(partial_sum, "tensor", scatter_dimension=1, tiled=True).astype(
        jnp.bfloat16
    )
    features = joined.shape[1]
    joined = jnp.dot(
        slot_table.astype(jnp.bfloat16),
        joined.reshape(count_all, TREE_SLOTS * features),
        preferred_element_type=jnp.float32,
    ).reshape(rows_all, features)
    scaled = (joined * norm_gain.astype(jnp.float32)).astype(jnp.bfloat16)
    partial_qkv = jnp.dot(scaled, qkv_weight, preferred_element_type=jnp.float32)
    row_squares = jnp.sum(joined * joined, axis=1)
    own_qkv = lax.psum_scatter(partial_qkv, "req", scatter_dimension=0, tiled=True)
    total_squares = lax.dynamic_slice_in_dim(
        lax.psum(row_squares, ("req", "tensor")),
        req_here * request_per_owner * TREE_SLOTS,
        request_per_owner * TREE_SLOTS,
    )
    total_qkv = lax.psum(own_qkv, "tensor")
    query_key_value = (total_qkv * lax.rsqrt(total_squares[:, None] / DF + norm_eps)).astype(
        jnp.bfloat16
    )
    query_group_width = QUERY_HEADS // KEY_VALUE_HEADS
    query_rows = query_key_value[:, : QUERY_HEADS * HEAD_SIZE].reshape(
        request_per_owner, TREE_SLOTS, KEY_VALUE_HEADS, query_group_width, HEAD_SIZE
    )
    fresh_key = query_key_value[
        :, QUERY_HEADS * HEAD_SIZE : (QUERY_HEADS + KEY_VALUE_HEADS) * HEAD_SIZE
    ].reshape(request_per_owner, TREE_SLOTS, KEY_VALUE_HEADS, HEAD_SIZE)
    fresh_value = query_key_value[:, (QUERY_HEADS + KEY_VALUE_HEADS) * HEAD_SIZE :].reshape(
        request_per_owner, TREE_SLOTS, KEY_VALUE_HEADS, HEAD_SIZE
    )
    cached_key_rows = owner_draft_cache[:, :, 0].reshape(
        request_per_owner, CACHE_BLOCK, KEY_VALUE_HEADS, HEAD_SIZE
    )
    cached_value_rows = owner_draft_cache[:, :, 1].reshape(
        request_per_owner, CACHE_BLOCK, KEY_VALUE_HEADS, HEAD_SIZE
    )
    lengths = lax.dynamic_slice_in_dim(cache_len, req_here * request_per_owner, request_per_owner)
    live_all = jnp.sum(jnp.where(slot_table, node_count[None, :], 0), axis=1)
    live_slot = lax.dynamic_slice_in_dim(live_all, req_here * request_per_owner, request_per_owner)
    scale_factor = HEAD_SIZE ** (-0.5)
    positions = tensor_here * CACHE_BLOCK + jnp.arange(CACHE_BLOCK)
    cache_mask = (positions[None, :] < lengths[:, None])[:, None, None, None, :]
    score_cache = (
        jnp.einsum(
            "snkgd,spkd->snkgp", query_rows, cached_key_rows, preferred_element_type=jnp.float32
        )
        * scale_factor
    )
    score_cache = jnp.where(cache_mask, score_cache, -1e30)
    first_block = tensor_here == 0
    new_mask = (jnp.arange(TREE_SLOTS)[None, :] <= jnp.arange(TREE_SLOTS)[:, None]) & first_block
    new_mask = new_mask[None, :, None, None, :]
    score_new = (
        jnp.einsum("snkgd,smkd->snkgm", query_rows, fresh_key, preferred_element_type=jnp.float32)
        * scale_factor
    )
    score_new = jnp.where(new_mask, score_new, -1e30)
    local_top = jnp.maximum(jnp.max(score_cache, axis=-1), jnp.max(score_new, axis=-1))
    top_score = lax.pmax(local_top, "tensor")
    weight_cache = jnp.where(cache_mask, jnp.exp(score_cache - top_score[..., None]), 0.0)
    weight_new = jnp.where(new_mask, jnp.exp(score_new - top_score[..., None]), 0.0)
    denominator = jnp.sum(weight_cache, axis=-1) + jnp.sum(weight_new, axis=-1)
    accum = jnp.einsum(
        "snkgp,spkd->snkgd",
        weight_cache.astype(jnp.bfloat16),
        cached_value_rows,
        preferred_element_type=jnp.float32,
    )
    accum = accum + jnp.einsum(
        "snkgm,smkd->snkgd",
        weight_new.astype(jnp.bfloat16),
        fresh_value,
        preferred_element_type=jnp.float32,
    )
    head_cols = QUERY_HEADS * HEAD_SIZE // tensor_count
    accum_all, denom_all = lax.psum((accum, denominator), "tensor")
    result_all = (accum_all / denom_all[..., None]).reshape(
        request_per_owner, TREE_SLOTS, QUERY_HEADS * HEAD_SIZE
    )
    result = lax.dynamic_slice_in_dim(result_all, tensor_here * head_cols, head_cols, 2)
    alive = (jnp.arange(TREE_SLOTS)[None, :] < live_slot[:, None])[:, :, None]
    return jnp.where(alive, result, 0.0).astype(jnp.bfloat16)


def solution(mesh):
    return jax.shard_map(
        body,
        mesh=mesh,
        in_specs=(
            P(("groups", "req"), "tensor"),
            P("tensor", "req"),
            P(("req", "tensor")),
            P(("req", "tensor"), None),
            P(("groups", "req"), "tensor", None, None),
            P("groups"),
            P("groups"),
            P("groups"),
        ),
        out_specs=P(("groups", "req"), None, "tensor"),
        check_vma=False,
    )
```

profile of v0, /device:TPU:0, one launch (start us, length us, event | category | flops | bytes accessed | tf_op | source)
XLA Modules:
  0.0 341.3 jit_solution(7624498871045635591)
XLA Ops:
  6.5 0.7 all-gather.2.cloned.1.call-update
  7.3 28.4 %all-gather.2.cloned.1.call-done = bf16[192,6144]{1,0:T(8,128)(2,1)} async-done(((bf16[48,6144]{1,0:T(8,128)(2,1)}), bf16[192,6144]{1,0:T(8,128)(2,1)}) %all-gather.2.cloned.1.call-update) | async-done | bytes 2359312 | tf_op jit(solution)/shard_map/all_gather | solution.py:34
  35.7 12.3 %fusion.29 = f32[192,2048]{1,0:T(8,128)} fusion(bf16[192,6144]{1,0:T(8,128)(2,1)} %all-gather.2.cloned.1.call-done, bf16[6144,2048]{1,0:T(8,128)(2,1)} %param.9), kind=kOutput, calls=%fused_computation.50 | convolution fusion | flops 4831838208 | bytes 29097984 | tf_op jit(solution)/shard_map/dot_general | solution.py:35
  48.9 34.6 %reduce-scatter.3.cloned.1.call-done = f32[192,512]{1,0:T(8,128)} async-done(((f32[192,2048]{1,0:T(8,128)}), f32[192,512]{1,0:T(8,128)}) %reduce-scatter.3.cloned.1.call-update) | async-done | bytes 393232 | tf_op jit(solution)/shard_map/reduce_scatter | solution.py:36
  83.5 1.0 convert_element_type.26
  84.9 8.6 %fusion.19 = f32[192,9216]{1,0:T(8,128)} fusion(bf16[512,9216]{1,0:T(8,128)(2,1)} %param.11, f32[192,512]{1,0:T(8,128)S(1)} %reshape.91, f32[512]{0:T(512)S(1)} %convert_element_type.27), kind=kOutput, calls=%fused_computation.28 | convolution fusion | flops 1812135936 | bytes 16910336 | tf_op jit(solution)/shard_map/dot_general | solution.py:46
  93.6 62.7 %reduce-scatter.5.cloned.1.call-done = f32[48,9216]{1,0:T(8,128)} async-done(((f32[192,9216]{1,0:T(8,128)}), f32[48,9216]{1,0:T(8,128)}) %reduce-scatter.5.cloned.1.call-update) | async-done | bytes 1769488 | tf_op jit(solution)/shard_map/reduce_scatter | solution.py:48
  156.4 3.1 fusion.27
  159.5 4.7 %copy.33 = bf16[6,128,1,512]{1,3,0,2:T(8,128)(2,1)} copy(bf16[6,128,1,512]{3,2,1,0:T(2,128)(2,1)} %get-tuple-element.5) | data formatting | bytes 1572864
  164.1 2.6 copy.34
  167.0 34.1 %psum.29 = f32[192]{0:T(256)S(1)} all-reduce(f32[192]{0:T(256)S(1)} %multiply_reduce_fusion), channel_id=1, replica_groups=mesh['groups'=2,'req'=4,'tensor'=4] {'req','tensor'}, use_global_device_ids=true, to_apply=%region_6.7 | all-reduce | flops 192 | bytes 1536 | tf_op jit(solution)/shard_map/psum | solution.py:50
  201.2 34.3 %all-reduce.3.cloned.1.call-done = f32[48,9216]{1,0:T(8,128)} async-done(((f32[48,9216]{1,0:T(8,128)}), f32[48,9216]{1,0:T(8,128)}) %all-reduce.3.cloned.1.call-update) | async-done | bytes 1769488 | tf_op jit(solution)/shard_map/psum | solution.py:54
  235.5 1.6 multiply_convert_fusion
  237.2 2.0 fusion.28
  239.1 0.6 bitcast_reduce_fusion
  239.8 18.5 %pmax.7 = f32[6,8,4,16]{3,1,2,0:T(8,128)S(1)} all-reduce(f32[6,8,4,16]{3,1,2,0:T(8,128)S(1)} %max.5), channel_id=1, replica_groups=mesh['groups'=2,'req'=4,'tensor'=4] {'tensor'}, use_global_device_ids=true, to_apply=%region_9.10 | all-reduce | flops 3072 | bytes 24576 | tf_op jit(solution)/shard_map/pmax | solution.py:96
  258.3 1.7 fusion.6
  260.0 1.8 bitcast_add_fusion
  261.8 0.6 copy-done.5
  263.1 0.9 fusion.4
  264.0 21.0 %psum.31 = f32[6,8,4,16]{3,1,2,0:T(8,128)S(1)} all-reduce(f32[6,8,4,16]{3,1,2,0:T(8,128)S(1)} %add.56), channel_id=1, replica_groups=mesh['groups'=2,'req'=4,'tensor'=4] {'tensor'}, use_global_device_ids=true, to_apply=%region_13.14 | all-reduce | flops 3072 | bytes 24576 | tf_op jit(solution)/shard_map/psum | solution.py:113
  285.0 46.5 %all-reduce.5.cloned.1.call-done = f32[6,8,4,16,128]{4,3,1,2,0:T(8,128)} async-done(((f32[6,8,4,16,128]{4,3,1,2,0:T(8,128)}), f32[6,8,4,16,128]{4,3,1,2,0:T(8,128)}) %all-reduce.5.cloned.1.call-update) | async-done | bytes 1572880 | tf_op jit(solution)/shard_map/psum | solution.py:113
  331.5 1.9 broadcast_divide_fusion
  334.0 0.8 select_convert_fusion
  (41 shorter events, 3.0 us)
Async XLA Ops:
  6.5 29.2 %all-gather.2.cloned.1.call-start = ((), (), s32[]{:S(2)}) async-start(), calls=%async_computation.2 | async-start | bytes 2949120 | tf_op jit(solution)/shard_map/all_gather | solution.py:34
  7.3 76.3 %reduce-scatter.3.cloned.1.call-start = ((), (), s32[]{:S(2)}) async-start(), calls=%async_computation.3 | async-start | bytes 1966080 | tf_op jit(solution)/shard_map/reduce_scatter | solution.py:36
  48.0 0.7 copy-start.2
  48.0 0.7 copy-start.3
  48.1 108.2 %reduce-scatter.5.cloned.1.call-start = ((), (), s32[]{:S(2)}) async-start(), calls=%async_computation.4 | async-start | bytes 8847360 | tf_op jit(solution)/shard_map/reduce_scatter | solution.py:48
  93.6 62.8 %copy-start = (bf16[6,128,2,512]{3,2,1,0:T(2,128)(2,1)S(1)}, bf16[6,128,2,512]{3,2,1,0:T(2,128)(2,1)}, u32[]{:S(2)}) copy-start(bf16[6,128,2,512]{3,2,1,0:T(2,128)(2,1)} %param.12) | copy-start | bytes 4718596
  93.6 141.9 %all-reduce.3.cloned.1.call-start = ((), (), s32[]{:S(2)}) async-start(), calls=%async_computation.5 | async-start | bytes 3538944 | tf_op jit(solution)/shard_map/psum | solution.py:54
  156.3 175.2 %all-reduce.5.cloned.1.call-start = ((), (), s32[]{:S(2)}) async-start(), calls=%async_computation.6 | async-start | bytes 3145728 | tf_op jit(solution)/shard_map/psum | solution.py:113
  164.1 2.6 copy-start.4
  237.1 2.0 copy-start.1
  261.8 0.7 copy-start.5
Sparse Core Ops, SparseCore 0:
  8.9 26.7 all-gather.1
  48.2 35.2 reduce-scatter.2
  93.7 62.5 reduce-scatter.4
  158.7 76.7 all-reduce.2
  261.9 69.5 all-reduce.4
where the time goes:
time: 342 us; the launch traced here: 341 us
  waiting for transfers between devices  207 us (61%)
  blocking collectives  73.6 us (22%)
  matrix products  27.2 us (8%)
  between operations  13.3 us (4%)
  local copies, waits for them, and re-layouts  12.5 us (4%)
  other arithmetic  7.31 us (2%)
    reduce_scatter x1, waiting for transfers between devices, body(): lax.psum_scatter(partial_qkv, 'req', scatter_dimension=0, tiled=True)  62.7 us
    psum x1, waiting for transfers between devices, body(): accum_all, denom_all = lax.psum((accum, denominator), 'tensor')  46.5 us
    reduce_scatter x1, waiting for transfers between devices, body(): lax.psum_scatter(partial_sum, 'tensor', scatter_dimension=1, tiled=True)  34.6 us
    psum x1, waiting for transfers between devices, body(): total_qkv = lax.psum(own_qkv, 'tensor')  34.3 us
    psum x1, blocking collectives, body(): lax.psum(row_squares, ('req', 'tensor'))  34.1 us
    all_gather x1, waiting for transfers between devices, body(): hidden_all = lax.all_gather(hidden, 'req', axis=0, tiled=True)  28.4 us
    psum x1, blocking collectives, body(): accum_all, denom_all = lax.psum((accum, denominator), 'tensor')  21 us
    pmax x1, blocking collectives, body(): top_score = lax.pmax(local_top, 'tensor')  18.5 us
  transfers between devices with their start and end apart: 5, of which 5 were waited for; matrix products, arithmetic and copies ran while one was open for 4% of the time, Pallas kernels for 0%

commit v1 on v0

--- a/solution.py
+++ b/solution.py
@@ -10,6 +10,27 @@
 TREE_SLOTS = 8
 CACHE_BLOCK = 128
 norm_eps = 1e-05
+
+
+def load_hubs(frame_in, in_dim):
+    frame_in = jnp.moveaxis(frame_in, 0, in_dim)
+    aux = frame_in.shape
+    return frame_in.reshape(*aux[:in_dim], aux[in_dim] * aux[in_dim + 1], *aux[in_dim + 2 :])
+
+
+def report_streams(x_local, axis_key):
+    t1, piece_next = (jax.lax.axis_size(axis_key), jax.lax.axis_index(axis_key))
+    t_next, value_now = (x_local[None], 1)
+    while value_now < t1:
+        current_block = jax.lax.ppermute(
+            t_next, axis_name=axis_key, perm=[(m, m ^ value_now) for m in range(t1)]
+        )
+        before = piece_next & value_now == 0
+        t_next = jnp.concatenate(
+            [jnp.where(before, t_next, current_block), jnp.where(before, current_block, t_next)]
+        )
+        value_now *= 2
+    return t_next
 
 
 def slots(owner, request_per_owner):
@@ -31,7 +52,7 @@
     slot_of = slots(owner, request_per_owner)
     slot_table = slot_of[None, :] == jnp.arange(count_all, dtype=jnp.int32)[:, None]
     rows_all = count_all * TREE_SLOTS
-    hidden_all = lax.all_gather(hidden, "req", axis=0, tiled=True)
+    hidden_all = load_hubs(report_streams(hidden, "req"), 0)
     partial_sum = jnp.dot(hidden_all, join_weight, preferred_element_type=jnp.float32)
     joined = lax.psum_scatter(partial_sum, "tensor", scatter_dimension=1, tiled=True).astype(
         jnp.bfloat16

time: 342 us -> 347 us (1.015)
    all_gather x1 -> x0, waiting for transfers between devices: 28.4 us -> none  [body(): hidden_all = lax.all_gather(hidden, 'req', axis=0, tiled=True)]
    ppermute x0 -> x2, waiting for transfers between devices: none -> 28.1 us  [report_streams(): jax.lax.ppermute(t_next, axis_name=axis_key, perm=[(m, m ^ value_now) for...]
  transfers between devices with their start and end apart: 5 -> 6, of which waited for: 5 -> 6; matrix products, arithmetic and copies ran while one was open for 4% -> 4% of each run, Pallas kernels for 0% -> 0%
where the time goes in v1:
time: 347 us
  waiting for transfers between devices  208 us (60%)
  blocking collectives  73.5 us (21%)
  matrix products  26.9 us (8%)
  between operations  13.3 us (4%)
  local copies, waits for them, and re-layouts  12.5 us (4%)
  other arithmetic  8.92 us (3%)
  starting transfers between devices  3.5 us (1%)
    reduce_scatter x1, waiting for transfers between devices, body(): lax.psum_scatter(partial_qkv, 'req', scatter_dimension=0, tiled=True)  62.7 us
    psum x1, waiting for transfers between devices, body(): accum_all, denom_all = lax.psum((accum, denominator), 'tensor')  46.5 us
    reduce_scatter x1, waiting for transfers between devices, body(): lax.psum_scatter(partial_sum, 'tensor', scatter_dimension=1, tiled=True)  36.1 us
    psum x1, waiting for transfers between devices, body(): total_qkv = lax.psum(own_qkv, 'tensor')  34.5 us
    psum x1, blocking collectives, body(): lax.psum(row_squares, ('req', 'tensor'))  34.1 us
    ppermute x2, waiting for transfers between devices, report_streams(): jax.lax.ppermute(t_next, axis_name=axis_key, perm=[(m, m ^ value_now) for...  28.1 us
    psum x1, blocking collectives, body(): accum_all, denom_all = lax.psum((accum, denominator), 'tensor')  21 us
    pmax x1, blocking collectives, body(): top_score = lax.pmax(local_top, 'tensor')  18.5 us
  transfers between devices with their start and end apart: 6, of which 6 were waited for; matrix products, arithmetic and copies ran while one was open for 4% of the time, Pallas kernels for 0%

profile of v1, /device:TPU:0, one launch (start us, length us, event | category | flops | bytes accessed | tf_op | source)
XLA Modules:
  0.0 346.6 jit_solution(164357499398489799)
XLA Ops:
  7.0 1.8 collective-permute-done
  8.8 1.1 broadcast_select_fusion.3
  10.1 2.9 collective-permute-start.1
  13.0 26.3 %collective-permute-done.1 = bf16[2,48,6144]{2,1,0:T(8,128)(2,1)S(1)} collective-permute-done((bf16[2,48,6144]{2,1,0:T(8,128)(2,1)S(1)}, bf16[2,48,6144]{2,1,0:T(8,128)(2,1)S(1)}, u32[]{:S(2)}, u32[]{:S(2)}) %collective-permute-start.1) | collective-permute-done | bytes 1179680 | tf_op jit(solution)/shard_map/ppermute | solution.py:25
  39.7 12.0 %fusion.29 = f32[192,2048]{1,0:T(8,128)} fusion(bf16[192,6144]{1,0:T(8,128)(2,1)S(1)} %bitcast.63, bf16[6144,2048]{1,0:T(8,128)(2,1)} %param.9), kind=kOutput, calls=%fused_computation.56 | convolution fusion | flops 4831838208 | bytes 29097984 | tf_op jit(solution)/shard_map/dot_general | solution.py:56
  52.5 36.1 %reduce-scatter.3.cloned.1.call-done = f32[192,512]{1,0:T(8,128)} async-done(((f32[192,2048]{1,0:T(8,128)}), f32[192,512]{1,0:T(8,128)}) %reduce-scatter.3.cloned.1.call-update) | async-done | bytes 393232 | tf_op jit(solution)/shard_map/reduce_scatter | solution.py:57
  88.6 1.0 convert_element_type.26
  90.0 8.6 %fusion.19 = f32[192,9216]{1,0:T(8,128)} fusion(bf16[512,9216]{1,0:T(8,128)(2,1)} %param.11, f32[192,512]{1,0:T(8,128)S(1)} %reshape.95, f32[512]{0:T(512)S(1)} %convert_element_type.27), kind=kOutput, calls=%fused_computation.34 | convolution fusion | flops 1812135936 | bytes 16910336 | tf_op jit(solution)/shard_map/dot_general | solution.py:67
  98.7 62.7 %reduce-scatter.5.cloned.1.call-done = f32[48,9216]{1,0:T(8,128)} async-done(((f32[192,9216]{1,0:T(8,128)}), f32[48,9216]{1,0:T(8,128)}) %reduce-scatter.5.cloned.1.call-update) | async-done | bytes 1769488 | tf_op jit(solution)/shard_map/reduce_scatter | solution.py:69
  161.5 3.1 fusion.27
  164.6 4.7 %copy.33 = bf16[6,128,1,512]{1,3,0,2:T(8,128)(2,1)} copy(bf16[6,128,1,512]{3,2,1,0:T(2,128)(2,1)} %get-tuple-element.7) | data formatting | bytes 1572864
  169.2 2.6 copy.34
  172.1 34.1 %psum.29 = f32[192]{0:T(256)S(1)} all-reduce(f32[192]{0:T(256)S(1)} %multiply_reduce_fusion), channel_id=1, replica_groups=mesh['groups'=2,'req'=4,'tensor'=4] {'req','tensor'}, use_global_device_ids=true, to_apply=%region_6.7 | all-reduce | flops 192 | bytes 1536 | tf_op jit(solution)/shard_map/psum | solution.py:71
  206.3 34.5 %all-reduce.3.cloned.1.call-done = f32[48,9216]{1,0:T(8,128)} async-done(((f32[48,9216]{1,0:T(8,128)}), f32[48,9216]{1,0:T(8,128)}) %all-reduce.3.cloned.1.call-update) | async-done | bytes 1769488 | tf_op jit(solution)/shard_map/psum | solution.py:75
  240.7 1.6 multiply_convert_fusion
  242.4 2.0 fusion.28
  245.1 18.5 %pmax.7 = f32[6,8,4,16]{3,1,2,0:T(8,128)S(1)} all-reduce(f32[6,8,4,16]{3,1,2,0:T(8,128)S(1)} %max.5), channel_id=1, replica_groups=mesh['groups'=2,'req'=4,'tensor'=4] {'tensor'}, use_global_device_ids=true, to_apply=%region_9.10 | all-reduce | flops 3072 | bytes 24576 | tf_op jit(solution)/shard_map/pmax | solution.py:117
  263.6 1.7 fusion.6
  265.3 1.8 bitcast_add_fusion
  268.4 0.9 fusion.4
  269.3 21.0 %psum.31 = f32[6,8,4,16]{3,1,2,0:T(8,128)S(1)} all-reduce(f32[6,8,4,16]{3,1,2,0:T(8,128)S(1)} %add.56), channel_id=1, replica_groups=mesh['groups'=2,'req'=4,'tensor'=4] {'tensor'}, use_global_device_ids=true, to_apply=%region_13.14 | all-reduce | flops 3072 | bytes 24576 | tf_op jit(solution)/shard_map/psum | solution.py:134
  290.3 46.5 %all-reduce.5.cloned.1.call-done = f32[6,8,4,16,128]{4,3,1,2,0:T(8,128)} async-done(((f32[6,8,4,16,128]{4,3,1,2,0:T(8,128)}), f32[6,8,4,16,128]{4,3,1,2,0:T(8,128)}) %all-reduce.5.cloned.1.call-update) | async-done | bytes 1572880 | tf_op jit(solution)/shard_map/psum | solution.py:134
  336.8 1.9 broadcast_divide_fusion
  339.3 0.8 select_convert_fusion
  (46 shorter events, 5.2 us)
Async XLA Ops:
  6.5 82.1 %reduce-scatter.3.cloned.1.call-start = ((), (), s32[]{:S(2)}) async-start(), calls=%async_computation.2 | async-start | bytes 1966080 | tf_op jit(solution)/shard_map/reduce_scatter | solution.py:57
  6.5 2.3 collective-permute-start
  10.1 29.2 %collective-permute-start.1 = (bf16[2,48,6144]{2,1,0:T(8,128)(2,1)S(1)}, bf16[2,48,6144]{2,1,0:T(8,128)(2,1)S(1)}, u32[]{:S(2)}, u32[]{:S(2)}) collective-permute-start(bf16[2,48,6144]{2,1,0:T(8,128)(2,1)S(1)} %pad_maximum_fusion.1), channel_id=1, source_target_pairs={{0,8},{4,12},{8,0},{12,4},{1,9},{5,13},{9,1},{13,5},{2,10},{6,14},... | collective-permute-start | bytes 3538952 | tf_op jit(solution)/shard_map/ppermute | solution.py:25
  51.7 0.7 copy-start.2
  51.7 0.7 copy-start.3
  51.7 109.7 %reduce-scatter.5.cloned.1.call-start = ((), (), s32[]{:S(2)}) async-start(), calls=%async_computation.3 | async-start | bytes 8847360 | tf_op jit(solution)/shard_map/reduce_scatter | solution.py:69
  98.7 62.8 %copy-start = (bf16[6,128,2,512]{3,2,1,0:T(2,128)(2,1)S(1)}, bf16[6,128,2,512]{3,2,1,0:T(2,128)(2,1)}, u32[]{:S(2)}) copy-start(bf16[6,128,2,512]{3,2,1,0:T(2,128)(2,1)} %param.12) | copy-start | bytes 4718596
  98.7 142.0 %all-reduce.3.cloned.1.call-start = ((), (), s32[]{:S(2)}) async-start(), calls=%async_computation.4 | async-start | bytes 3538944 | tf_op jit(solution)/shard_map/psum | solution.py:75
  161.4 175.4 %all-reduce.5.cloned.1.call-start = ((), (), s32[]{:S(2)}) async-start(), calls=%async_computation.5 | async-start | bytes 3145728 | tf_op jit(solution)/shard_map/psum | solution.py:134
  169.2 2.6 copy-start.4
  242.4 2.0 copy-start.1
  267.1 0.7 copy-start.5
Sparse Core Ops, SparseCore 0:
  51.8 36.7 reduce-scatter.2
  98.8 62.5 reduce-scatter.4
  163.9 76.7 all-reduce.2
  267.2 69.5 all-reduce.4
